TPU v7x, 512 devices: a whole 4x4x16 slice. The times are simulated.
512 devices in a mesh: group: 8 (over z_lo, core), ctx: 64 (over x, y, z_hi).
Axes of the slice: x: 4, y: 4, z: 16 (z_hi: 4, z_lo: 4; z = z_hi * 4 + z_lo), core: 2. Of those that a mesh axis runs over, the one named last changes fastest.
Arguments:
- queries: bfloat16 [8192, 4096], P(('group', 'ctx')), may hold values from -16 to 16
- key_states: bfloat16 [8192, 4096], P(('group', 'ctx')), may hold values from -16 to 16
- value_states: bfloat16 [8192, 4096], P(('group', 'ctx')), may hold values from -6 to 6
- gate_table: float32 [32, 4096], replicated, may hold values from 0.3 to 3
- noise_levels: int32 [8], replicated, may hold values from 0 to 31
- group_ids: int32 [8], replicated, may hold values from 0 to 7, each once
Outputs:
- handed: bfloat16 [8192, 4096], P(('group', 'ctx'))
Inputs may be any that keep to these rules, and one draw needn't show every extreme that they name: `group_ids`: each of 0 to 7 appears once.
All inputs are finite; a program needn't handle non-finite values.
Results may differ from a plain program's by a relative error of at most 0.007.
Values may be sent and summed in bfloat16 or wider, within the bound.
A program may use at most 64 MiB of HBM per device.

v0:
```python
import jax
import jax.numpy as jnp
from jax import lax
from jax.sharding import PartitionSpec as P

HEADS = 32
HEAD = 128


def shifted(block, axis, distance):
    devices = range(lax.axis_size(axis))
    route = [((i - distance) % len(devices), i) for i in devices]
    return lax.ppermute(block, axis, route)


def doubled(states):
    row_count = states.shape[0]
    shaped = states.reshape(row_count, HEADS, 1, HEAD)
    return jnp.broadcast_to(shaped, (row_count, HEADS, 2, HEAD)).reshape(row_count, 2 * HEADS, HEAD)


def attend(running, chosen, key_block, value_block, key_group, group_ids, own_id):
    peak, total, summed = running
    marked = key_group[:, None] == jnp.arange(group_ids.shape[0], dtype=jnp.int32)[None, :]
    key_ids = jnp.sum(jnp.where(marked, group_ids[None, :], 0), axis=1)
    allowed = (key_ids <= own_id)[None, None, :]
    scores = jnp.einsum("pqd,rpd->pqr", chosen, key_block, preferred_element_type=jnp.float32)
    scores = jnp.where(allowed, scores * (1.0 / HEAD**0.5), -1e30)
    new_peak = jnp.maximum(peak, jnp.max(scores, axis=-1))
    weights = jnp.where(allowed, jnp.exp(scores - new_peak[..., None]), 0.0)
    total = jnp.sum(weights, axis=-1)
    summed = jnp.einsum(
        "pqr,rpd->pqd",
        weights.astype(jnp.bfloat16),
        value_block,
        preferred_element_type=jnp.float32,
    )
    return (new_peak, total, summed)


def local(queries, key_states, value_states, gate_table, noise_levels, group_ids):
    tok_count = queries.shape[0]
    ctx_count = lax.axis_size("ctx")
    group_count = lax.axis_size("group")
    slot_count = 2 * HEADS // ctx_count
    group_rows = tok_count * ctx_count
    half_rows = group_rows // 2
    section_marks = jnp.arange(group_count, dtype=jnp.int32) == lax.axis_index("group")
    own_id = jnp.sum(jnp.where(section_marks, group_ids, 0))
    own_level = jnp.sum(jnp.where(section_marks, noise_levels, 0))
    slot_index = lax.axis_index("ctx") * slot_count + jnp.arange(slot_count, dtype=jnp.int32)
    offsets = slot_index % 2 * half_rows

    def select(offset, block):
        return lax.dynamic_slice_in_dim(block, offset, half_rows, 0)

    initial = (
        jnp.full((slot_count, half_rows), -1e30, jnp.float32),
        jnp.zeros((slot_count, half_rows), jnp.float32),
        jnp.zeros((slot_count, half_rows, HEAD), jnp.float32),
    )
    query_heads, key_heads, value_heads = (
        lax.all_to_all(doubled(queries), "ctx", split_axis=1, concat_axis=0, tiled=True),
        lax.all_to_all(doubled(key_states), "ctx", split_axis=1, concat_axis=0, tiled=True),
        lax.all_to_all(doubled(value_states), "ctx", split_axis=1, concat_axis=0, tiled=True),
    )
    chosen = jax.vmap(select, in_axes=(0, 1))(offsets, query_heads)
    key_piece = lax.all_gather(key_heads, "group", axis=0, tiled=True)
    value_piece = lax.all_gather(value_heads, "group", axis=0, tiled=True)
    key_group = jnp.arange(key_piece.shape[0], dtype=jnp.int32) // group_rows
    running = attend(initial, chosen, key_piece, value_piece, key_group, group_ids, own_id)
    peak, total, summed = running
    attended = (summed / total[..., None]).astype(jnp.bfloat16)

    def place(offset, block):
        return lax.dynamic_update_slice_in_dim(
            jnp.zeros((group_rows, HEAD), jnp.bfloat16), block, offset, 0
        )

    spread = jax.vmap(place, out_axes=1)(offsets, attended)
    returned = lax.all_to_all(spread, "ctx", split_axis=0, concat_axis=1, tiled=True)
    paired = returned.reshape(tok_count, HEADS, 2, HEAD)
    merged = (paired[:, :, 0] + paired[:, :, 1]).reshape(tok_count, HEADS * HEAD)
    level_marks = jnp.arange(gate_table.shape[0], dtype=jnp.int32)[:, None] == own_level
    gate_row = jnp.sum(jnp.where(level_marks, gate_table, 0.0), axis=0)
    done = (merged.astype(jnp.float32) * gate_row[None, :]).astype(jnp.bfloat16)
    return shifted(done, "group", 1)


def solution(mesh):
    placed = (
        P(("group", "ctx"), None),
        P(("group", "ctx"), None),
        P(("group", "ctx"), None),
        P(),
        P(),
        P(),
    )
    return jax.shard_map(
        local, mesh=mesh, in_specs=placed, out_specs=P(("group", "ctx"), None), check_vma=False
    )
```

profile of v0, /device:TPU:1, one launch (start us, length us, event | category | flops | bytes accessed | tf_op | source)
XLA Modules:
  0.0 210.4 jit_solution(10687570617880946759)
XLA Ops:
  6.5 0.0 copy-start
  6.5 0.0 all-gather.3.cloned.1.call-start
  6.5 0.9 copy-done
  7.5 39.8 %all_to_all.66 = bf16[16,64,128]{2,0,1:T(8,128)(2,1)} all-to-all(bf16[16,64,128]{2,0,1:T(8,128)(2,1)S(1)} %bitcast.78), channel_id=1, replica_groups=mesh['group'=8,'ctx'=64] {'ctx'}, dimensions={1} | all-to-all | bytes 524288 | tf_op jit(solution)/shard_map/all_to_all | solution.py:64
  47.3 0.0 all-gather.3.cloned.1.call-update
  47.4 0.0 all-gather.5.cloned.1.call-start
  47.4 0.9 copy_bitcast_fusion
  48.4 25.2 %all_to_all.67 = bf16[16,64,128]{2,0,1:T(8,128)(2,1)} all-to-all(bf16[16,64,128]{2,0,1:T(8,128)(2,1)S(1)} %bitcast.79), channel_id=1, replica_groups=mesh['group'=8,'ctx'=64] {'ctx'}, dimensions={1} | all-to-all | bytes 524288 | tf_op jit(solution)/shard_map/all_to_all | solution.py:65
  73.6 0.0 all-gather.5.cloned.1.call-update
  73.6 0.9 copy_bitcast_fusion.2
  74.6 0.7 broadcast_in_dim.90
  75.3 4.8 %all-to-all-start = ((bf16[16,64,128]{2,0,1:T(8,128)(2,1)}), bf16[16,64,128]{2,0,1:T(8,128)(2,1)S(1)}, u32[]{:S(2)}, u32[]{:S(2)}) async-start(bf16[16,64,128]{2,0,1:T(8,128)(2,1)} %bitcast.4), calls=%async_computation | async-start | bytes 524288 | tf_op jit(solution)/shard_map/all_to_all | solution.py:63
  80.1 0.7 add_clamp_fusion
  80.9 0.6 fusion.42
  81.5 1.4 fusion.36
  82.8 2.6 %and_reduce_fusion = pred[]{:T(512)} fusion(s32[3]{0:T(128)} %constant.87.clone.1, s32[1]{0:T(128)} %bitcast.3, s32[1]{0:T(128)} %bitcast.2, s32[1]{0:T(128)} %constant.79.clone.1), kind=kLoop, calls=%fused_computation.35 | loop fusion | flops 17 | bytes 25 | tf_op jit(solution)/shard_map/reduce.1
  85.4 0.8 select_reduce_fusion.1
  86.2 0.6 broadcast_compare_fusion
  86.9 13.1 %all-to-all-done = bf16[16,64,128]{2,0,1:T(8,128)(2,1)S(1)} async-done(((bf16[16,64,128]{2,0,1:T(8,128)(2,1)}), bf16[16,64,128]{2,0,1:T(8,128)(2,1)S(1)}, u32[]{:S(2)}, u32[]{:S(2)}) %all-to-all-start) | async-done | bytes 262176 | tf_op jit(solution)/shard_map/all_to_all | solution.py:63
  100.0 1.1 all-gather.3.cloned.1.call-done
  101.1 4.2 %fusion = (f32[512]{0:T(512)S(1)}, f32[512,8192]{1,0:T(8,128)S(1)}) fusion(pred[8192]{0:T(1024)(128)(4,1)S(1)} %broadcast_compare_fusion, bf16[8192,1,128]{2,0,1:T(8,128)(2,1)} %all-gather.3.cloned.1.call-done, bf16[1,1024,128]{2,1,0:T(8,128)(2,1)S(1)} %bitcast.80, s32[]{:T(128)} %bitcast.8), kind=kOutput, calls=%fused_computation.2 | convolution fusion | flops 1086324224 | bytes 19015684 | tf_op jit(solution)/shard_map/pqd,rpd->pqr/dot_general | solution.py:27
  105.3 0.0 copy-start.1
  105.3 5.7 %copy-done.1 = f32[512,8192]{1,0:T(8,128)} copy-done((f32[512,8192]{1,0:T(8,128)}, f32[512,8192]{1,0:T(8,128)S(1)}, u32[]{:S(2)}) %copy-start.1) | copy-done | bytes 16777240
  111.0 5.2 %fusion.1 = f32[512]{0:T(512)S(1)} fusion(f32[512,8192]{1,0:T(8,128)S(1)} %get-tuple-element.31, f32[512]{0:T(512)S(1)} %broadcast_maximum_fusion, pred[8192]{0:T(1024)(128)(4,1)S(1)} %broadcast_compare_fusion), kind=kLoop, calls=%fused_computation.3 | loop fusion | flops 20971008 | bytes 16789504 | tf_op jit(solution)/shard_map/reduce_sum | solution.py:31
  116.3 0.0 copy-start.3
  116.3 0.0 copy-start.2
  116.3 28.4 %all-gather.5.cloned.1.call-done = bf16[8192,1,128]{2,0,1:T(8,128)(2,1)} async-done(((bf16[1024,1,128]{2,0,1:T(8,128)(2,1)}), bf16[8192,1,128]{2,0,1:T(8,128)(2,1)}) %all-gather.5.cloned.1.call-update) | async-done | bytes 2097168 | tf_op jit(solution)/shard_map/all_gather | solution.py:69
  144.7 10.2 %fusion.24 = bf16[512,1,128]{2,0,1:T(8,128)(2,1)S(1)} fusion(bf16[8192,1,128]{2,0,1:T(8,128)(2,1)} %all-gather.5.cloned.1.call-done, f32[512,8192]{1,0:T(8,128)} %copy-done.1, f32[512]{0:T(512)S(1)} %broadcast_maximum_fusion, pred[8192]{0:T(1024)(128)(4,1)S(1)} %broadcast_compare_fusion, f32[512]{0:T(512)S(1)} %fusion.1, pred[]{:T(512)} %and_reduce_fusion), kind=kOutput, calls=%fused_computation.13 | convolution fusion | flops 1094909952 | bytes 19017728 | tf_op jit(solution)/shard_map/pqr,rpd->pqd/dot_general | solution.py:32
  154.9 0.3 broadcast_in_dim.84
  155.2 0.8 copy_dynamic-update-slice_fusion
  156.0 0.5 broadcast.129
  156.6 2.2 %reduce.12 = bf16[1024,128]{1,0:T(8,128)(2,1)S(1)} reduce(bf16[1024,1,128]{2,1,0:T(2,128)(2,1)S(1)} %copy_dynamic-update-slice_fusion, bf16[]{:T(256)} %broadcast.129), dimensions={1}, to_apply=%copy_dynamic-update-slice_fusion.reduce_sub_computation | reduce | bytes 524290 | tf_op jit(solution)/shard_map/vmap(vmap())/scatter | solution.py:76
  158.8 0.8 reshape.204
  159.5 15.8 %all-to-all-start.3 = ((bf16[64,2,1024]{2,1,0:T(2,128)(2,1)}), bf16[64,2,1024]{2,1,0:T(2,128)(2,1)S(1)}, u32[]{:S(2)}, u32[]{:S(2)}) async-start(bf16[64,2,1024]{2,1,0:T(2,128)(2,1)} %reshape.204), calls=%async_computation.3 | async-start | bytes 524288 | tf_op jit(solution)/shard_map/all_to_all | solution.py:81
  175.4 0.0 copy-done.3
  175.4 0.6 fusion.37
  176.0 0.6 iota_compare_fusion.1
  176.7 0.0 copy-done.2
  176.7 0.1 select_reduce_fusion
  176.8 19.8 %all-to-all-done.3 = bf16[64,2,1024]{2,1,0:T(2,128)(2,1)S(1)} async-done(((bf16[64,2,1024]{2,1,0:T(2,128)(2,1)}), bf16[64,2,1024]{2,1,0:T(2,128)(2,1)S(1)}, u32[]{:S(2)}, u32[]{:S(2)}) %all-to-all-start.3) | async-done | bytes 262176 | tf_op jit(solution)/shard_map/all_to_all | solution.py:81
  196.7 0.2 reshape.205
  197.0 0.1 copy.28
  197.0 0.2 fusion.29
  197.2 3.7 %collective-permute-start = (bf16[16,4096]{1,0:T(8,128)(2,1)S(1)}, bf16[16,4096]{1,0:T(8,128)(2,1)S(1)}, u32[]{:S(2)}, u32[]{:S(2)}) collective-permute-start(bf16[16,4096]{1,0:T(8,128)(2,1)S(1)} %fusion.29), channel_id=1, source_target_pairs={{448,0},{0,64},{64,128},{128,192},{192,256},{256,320},{320,384},{3... | collective-permute-start | bytes 393224 | tf_op jit(solution)/shard_map/ppermute | solution.py:13
  201.0 1.9 collective-permute-done
  202.9 0.7 copy.41
  (7 shorter events, 0.2 us)
Async XLA Ops:
  6.5 0.9 copy-start
  6.5 94.6 %all-gather.3.cloned.1.call-start = ((), (), s32[]{:S(2)}) async-start(), calls=%async_computation.4 | async-start | bytes 2359296 | tf_op jit(solution)/shard_map/all_gather | solution.py:68
  47.4 97.3 %all-gather.5.cloned.1.call-start = ((), (), s32[]{:S(2)}) async-start(), calls=%async_computation.5 | async-start | bytes 2359296 | tf_op jit(solution)/shard_map/all_gather | solution.py:69
  75.3 24.7 %all-to-all-start = ((bf16[16,64,128]{2,0,1:T(8,128)(2,1)}), bf16[16,64,128]{2,0,1:T(8,128)(2,1)S(1)}, u32[]{:S(2)}, u32[]{:S(2)}) async-start(bf16[16,64,128]{2,0,1:T(8,128)(2,1)} %bitcast.4), calls=%async_computation | async-start | bytes 524288 | tf_op jit(solution)/shard_map/all_to_all | solution.py:63
  105.3 5.7 %copy-start.1 = (f32[512,8192]{1,0:T(8,128)}, f32[512,8192]{1,0:T(8,128)S(1)}, u32[]{:S(2)}) copy-start(f32[512,8192]{1,0:T(8,128)S(1)} %get-tuple-element.31) | copy-start | bytes 50331652
  116.3 59.1 %copy-start.3 = (s32[8]{0:T(128)S(1)}, s32[8]{0:T(128)}, u32[]{:S(2)}) copy-start(s32[8]{0:T(128)} %param.12) | copy-start | bytes 100
  116.3 60.4 %copy-start.2 = (f32[32,4096]{1,0:T(8,128)S(1)}, f32[32,4096]{1,0:T(8,128)}, u32[]{:S(2)}) copy-start(f32[32,4096]{1,0:T(8,128)} %param.11) | copy-start | bytes 1572868
  159.5 37.1 %all-to-all-start.3 = ((bf16[64,2,1024]{2,1,0:T(2,128)(2,1)}), bf16[64,2,1024]{2,1,0:T(2,128)(2,1)S(1)}, u32[]{:S(2)}, u32[]{:S(2)}) async-start(bf16[64,2,1024]{2,1,0:T(2,128)(2,1)} %reshape.204), calls=%async_computation.3 | async-start | bytes 524288 | tf_op jit(solution)/shard_map/all_to_all | solution.py:81
  197.2 5.7 %collective-permute-start = (bf16[16,4096]{1,0:T(8,128)(2,1)S(1)}, bf16[16,4096]{1,0:T(8,128)(2,1)S(1)}, u32[]{:S(2)}, u32[]{:S(2)}) collective-permute-start(bf16[16,4096]{1,0:T(8,128)(2,1)S(1)} %fusion.29), channel_id=1, source_target_pairs={{448,0},{0,64},{64,128},{128,192},{192,256},{256,320},{320,384},{3... | collective-permute-start | bytes 393224 | tf_op jit(solution)/shard_map/ppermute | solution.py:13
Sparse Core Ops, SparseCore 0:
  47.5 53.6 all-gather.2
  103.2 41.4 all-gather.4
where the time goes:
time: 214 us; the launch traced here: 210 us
  blocking collectives  65 us (30%)
  waiting for transfers between devices  64.4 us (30%)
  starting transfers between devices  24.4 us (11%)
  other arithmetic  15.2 us (7%)
  matrix products  14.4 us (7%)
  between operations  13.6 us (6%)
  local copies, waits for them, and re-layouts  13.3 us (6%)
    all_to_all x1, blocking collectives, local(): lax.all_to_all(doubled(key_states), 'ctx', split_axis=1, concat_axis=0, t...  39.8 us
    all_gather x1, waiting for transfers between devices, local(): value_piece = lax.all_gather(value_heads, 'group', axis=0, tiled=True)  28.4 us
    all_to_all x1, blocking collectives, local(): lax.all_to_all(doubled(value_states), 'ctx', split_axis=1, concat_axis=0,...  25.2 us
    all_to_all x1, waiting for transfers between devices, local(): lax.all_to_all(spread, 'ctx', split_axis=0, concat_axis=1, tiled=True)  19.8 us
    all_to_all x1, starting transfers between devices, local(): lax.all_to_all(spread, 'ctx', split_axis=0, concat_axis=1, tiled=True)  15.8 us
    all_to_all x1, waiting for transfers between devices, local(): lax.all_to_all(doubled(queries), 'ctx', split_axis=1, concat_axis=0, tile...  13.1 us
    dot_general x1, matrix products, attend(): jnp.einsum('pqr,rpd->pqd', weights.astype(jnp.bfloat16), value_block, pre...  10.2 us
    unnamed x12, local copies, waits for them, and re-layouts  8.27 us
  transfers between devices with their start and end apart: 5, of which 5 were waited for; matrix products, arithmetic and copies ran while one was open for 10% of the time, Pallas kernels for 0%

commit v1 on v0

v1 whole, which is shorter than its diff:
```python
import functools
import math

import jax
import jax.numpy as jnp
from jax import lax
from jax.experimental import pallas as pl
from jax.experimental.pallas import tpu as pltpu
from jax.sharding import PartitionSpec as P

HEADS = 32
HEAD = 128
GROUPS = 8
TOK = 16
Z = 16
ZLO = 4
SIDE = 4
BLOCK = 256
PART = BLOCK // SIDE
SCALE = math.log2(math.e) / math.sqrt(HEAD)
MESH = pl.DeviceIdType.MESH
V_AFTER = (3, 5, 6, 7)
ORDER = (0, 3, 1, 2)


def kernel(
    levels_ref, ids_ref, q_ref, k_ref, v_ref, gate_ref, out_ref,
    q_in, k_in, v_in, gate, q_all, k_all, v_all, k_cat, v_cat, scores, weights,
    part_out, part_in, stat_out, stat_in, merged, final,
    load_sem, kz_sem, qz_sem, vz_sem, x_sem, y_sem, o_sem, s_sem, f_sem, send_sem,
):
    group, ctx = lax.axis_index("group"), lax.axis_index("ctx")
    zlo, core = group // 2, group % 2
    x, y, zhi = ctx // 16, ctx // 4 % 4, ctx % 4
    z = zhi * ZLO + zlo

    def device(x, y, z, core):
        return (z % ZLO * 2 + core, (x * SIDE + y) * 4 + z // ZLO)

    def column(head):
        return pl.ds(pl.multiple_of(head * HEAD, HEAD), HEAD)

    head = z * 2 + core
    loads = [
        pltpu.make_async_copy(k_ref, k_in, load_sem.at[0]),
        pltpu.make_async_copy(q_ref, q_in, load_sem.at[1]),
        pltpu.make_async_copy(v_ref, v_in, load_sem.at[2]),
        pltpu.make_async_copy(gate_ref.at[:, column(head)], gate, load_sem.at[3]),
    ]
    for load in loads:
        load.start()

    barrier = pltpu.get_barrier_semaphore()

    def greet_z(i, carry):
        pl.semaphore_signal(
            barrier, inc=1, device_id=device(x, y, (z + i // 2) % Z, (core + i) % 2), device_id_type=MESH
        )
        return carry

    lax.fori_loop(1, 2 * Z, greet_z, 0)
    for step in range(1, SIDE):
        pl.semaphore_signal(barrier, inc=1, device_id=device((x + step) % SIDE, y, z, core), device_id_type=MESH)
        pl.semaphore_signal(barrier, inc=1, device_id=device(x, (y + step) % SIDE, z, core), device_id_type=MESH)
    for load in loads:
        load.wait()
    pl.semaphore_wait(barrier, 2 * Z - 1 + 2 * (SIDE - 1))

    own = ((k_in, k_all, kz_sem, 0), (q_in, q_all, qz_sem, 1), (v_in, v_all, vz_sem, 2))
    for source, target, sem, number in own:
        pltpu.make_async_copy(source.at[:, column(head)], target.at[0, 0, 0, core], sem.at[0]).start()

        def send_z(i, carry, source=source, target=target, sem=sem, number=number):
            apart, other = i // 2, i % 2
            to_z, to_core = (z + Z - apart) % Z, (core + other) % 2
            pltpu.make_async_remote_copy(
                src_ref=source.at[:, column(to_z * 2 + to_core)],
                dst_ref=target.at[0, apart // ZLO, apart % ZLO, core],
                send_sem=send_sem.at[number],
                recv_sem=sem.at[apart // ZLO],
                device_id=device(x, y, to_z, to_core),
                device_id_type=MESH,
            ).start()
            return carry

        for chunk in ORDER:
            lax.fori_loop(max(1, 8 * chunk), 8 * chunk + 8, send_z, 0)

    def wait_bytes(ref, sem):
        pltpu.make_async_copy(ref, ref, sem).wait()

    def forward(buffer, chunk, arrived, along_x, send, receive):
        wait_bytes(buffer.at[0, chunk], arrived.at[chunk])
        for step in range(1, SIDE):
            if along_x:
                target = device((x + SIDE - step) % SIDE, y, z, core)
            else:
                target = device(x, (y + SIDE - step) % SIDE, z, core)
            pltpu.make_async_remote_copy(
                src_ref=buffer.at[0, chunk],
                dst_ref=buffer.at[step, chunk],
                send_sem=send,
                recv_sem=receive,
                device_id=target,
                device_id_type=MESH,
            ).start()

    for chunk in ORDER:
        forward(k_all, chunk, kz_sem, True, send_sem.at[3], x_sem.at[0])
    for chunk in ORDER:
        forward(q_all, chunk, qz_sem, False, send_sem.at[4], y_sem)
    wait_bytes(k_all.at[pl.ds(1, SIDE - 1)], x_sem.at[0])
    wait_bytes(q_all.at[pl.ds(1, SIDE - 1)], y_sem)

    def holder(rank):
        found = jnp.int32(0)
        for g in range(GROUPS):
            found = found + jnp.where(ids_ref[g] == rank, jnp.int32(g), jnp.int32(0))
        return found

    ranked = [holder(rank) for rank in range(GROUPS)]
    slots = [((g // 2 - zlo + ZLO) % ZLO, g % 2) for g in ranked]

    def block(buffer, rank):
        near, side = slots[rank]
        return buffer[:, :, near, side].reshape(BLOCK, HEAD)

    for rank in range(GROUPS):
        k_cat[pl.ds(rank * BLOCK, BLOCK), :] = block(k_all, rank)

    for rank in range(GROUPS):
        queries = block(q_all, rank)
        slot = rank % 2
        peak = None
        for other in range(rank + 1):
            keys = k_cat[pl.ds(other * BLOCK, BLOCK), :]
            product = lax.dot_general(
                queries, keys, (((1,), (1,)), ((), ())), preferred_element_type=jnp.float32
            )
            scores[slot, :, pl.ds(other * BLOCK, BLOCK)] = product
            high = jnp.maximum(product[:, :HEAD], product[:, HEAD:])
            peak = high if peak is None else jnp.maximum(peak, high)
        peak = jnp.max(peak, axis=1, keepdims=True)
        stat_out[1, rank] = jnp.broadcast_to(peak, (BLOCK, HEAD))
        for other in range(rank + 1):
            span = pl.ds(other * BLOCK, BLOCK)
            weights[rank, :, span] = jnp.exp2((scores[slot, :, span] - peak) * SCALE).astype(jnp.bfloat16)
        for chunk, after in zip(ORDER, V_AFTER):
            if after == rank:
                forward(v_all, chunk, vz_sem, True, send_sem.at[5], x_sem.at[1])

    wait_bytes(v_all.at[pl.ds(1, SIDE - 1)], x_sem.at[1])
    v_cat[:, HEAD:] = jnp.ones((GROUPS * BLOCK, HEAD), jnp.bfloat16)
    for rank in range(GROUPS):
        v_cat[pl.ds(rank * BLOCK, BLOCK), :HEAD] = block(v_all, rank)

    rows = lax.broadcasted_iota(jnp.int32, (HEAD, HEAD), 0)
    lanes = lax.broadcasted_iota(jnp.int32, (HEAD, HEAD), 1)
    diagonal = rows == lanes
    for rank in range(GROUPS):
        width = (rank + 1) * BLOCK
        product = jnp.dot(
            weights[rank, :, pl.ds(0, width)], v_cat[pl.ds(0, width), :], preferred_element_type=jnp.float32
        )
        total = product[:, HEAD:]
        part_out[rank] = (product[:, :HEAD] / total).astype(jnp.bfloat16).reshape(SIDE, PART, HEAD)
        logs = stat_out[1, rank] * SCALE + jnp.log2(total)
        for half in range(2):
            square = logs[half * HEAD : (half + 1) * HEAD]
            stat_in[0, pl.ds(2 * rank + half, 1), :] = jnp.sum(jnp.where(diagonal, square, 0.0), axis=0, keepdims=True)
        for step in range(1, SIDE):
            pltpu.make_async_remote_copy(
                src_ref=part_out.at[rank, step],
                dst_ref=part_in.at[step - 1, rank],
                send_sem=send_sem.at[6],
                recv_sem=o_sem,
                device_id=device(x, (y + step) % SIDE, z, core),
                device_id_type=MESH,
            ).start()
    for step in range(1, SIDE):
        pltpu.make_async_remote_copy(
            src_ref=stat_in.at[0],
            dst_ref=stat_in.at[step],
            send_sem=send_sem.at[7],
            recv_sem=s_sem,
            device_id=device(x, (y + step) % SIDE, z, core),
            device_id_type=MESH,
        ).start()
    wait_bytes(part_in, o_sem)
    wait_bytes(stat_in.at[pl.ds(1, SIDE - 1)], s_sem)

    part_rows = lax.broadcasted_iota(jnp.int32, (PART, HEAD), 0)
    part_lanes = lax.broadcasted_iota(jnp.int32, (PART, HEAD), 1)
    for rank in range(GROUPS):
        logs = []
        for step in range(SIDE):
            line = stat_in[step, pl.ds(2 * rank + step // 2, 1), :]
            picked = jnp.where(part_lanes == part_rows + step % 2 * PART, line, 0.0)
            logs.append(jnp.sum(picked, axis=1, keepdims=True))
        top = functools.reduce(jnp.maximum, logs)
        shares = [jnp.exp2(log - top) for log in logs]
        whole = functools.reduce(jnp.add, shares)
        value = part_out[rank, 0].astype(jnp.float32) * (shares[0] / whole)
        for step in range(1, SIDE):
            value = value + part_in[step - 1, rank].astype(jnp.float32) * (shares[step] / whole)
        merged[rank] = value.astype(jnp.bfloat16)

    for g in range(GROUPS):
        row = gate[pl.ds(levels_ref[g], 1), :]
        done = merged[ids_ref[g]].astype(jnp.float32) * row
        final[g] = done.astype(jnp.bfloat16).reshape(4, TOK, HEAD)

    def place(i):
        to_z, to_core = (z + i // 2) % Z, (core + i) % 2
        from_group = (to_z % ZLO * 2 + to_core + GROUPS - 1) % GROUPS
        from_z = to_z // ZLO * ZLO + from_group // 2
        return final.at[from_group, (from_z - z + Z) % Z // ZLO], device(x, y, to_z, to_core)

    tile, _ = place(0)
    pltpu.make_async_copy(tile, out_ref.at[:, column(head)], f_sem).start()

    def send_back(i, carry):
        tile, target = place(i)
        pltpu.make_async_remote_copy(
            src_ref=tile,
            dst_ref=out_ref.at[:, column(head)],
            send_sem=send_sem.at[8],
            recv_sem=f_sem,
            device_id=target,
            device_id_type=MESH,
        ).start()
        return carry

    lax.fori_loop(1, 2 * Z, send_back, 0)
    for number, source in enumerate((k_in, q_in, v_in)):
        wait_bytes(source.at[:, pl.ds(0, (2 * Z - 1) * HEAD)], send_sem.at[number])
    wait_bytes(k_all.at[pl.ds(1, SIDE - 1)], send_sem.at[3])
    wait_bytes(q_all.at[pl.ds(1, SIDE - 1)], send_sem.at[4])
    wait_bytes(v_all.at[pl.ds(1, SIDE - 1)], send_sem.at[5])
    wait_bytes(part_in, send_sem.at[6])
    wait_bytes(stat_in.at[pl.ds(1, SIDE - 1)], send_sem.at[7])
    wait_bytes(k_in.at[:, pl.ds(0, (2 * Z - 1) * HEAD)], send_sem.at[8])
    wait_bytes(out_ref, f_sem)


def local(queries, key_states, value_states, gate_table, noise_levels, group_ids):
    bf16, f32 = jnp.bfloat16, jnp.float32
    held = (SIDE, 4, ZLO, 2, TOK, HEAD)
    every = GROUPS * BLOCK
    return pl.pallas_call(
        kernel,
        out_shape=jax.ShapeDtypeStruct((TOK, HEADS * HEAD), bf16),
        in_specs=[pl.BlockSpec(memory_space=pltpu.SMEM)] * 2 + [pl.BlockSpec(memory_space=pl.ANY)] * 4,
        out_specs=pl.BlockSpec(memory_space=pltpu.VMEM),
        scratch_shapes=[
            pltpu.VMEM((TOK, HEADS * HEAD), bf16),
            pltpu.VMEM((TOK, HEADS * HEAD), bf16),
            pltpu.VMEM((TOK, HEADS * HEAD), bf16),
            pltpu.VMEM((32, HEAD), f32),
            pltpu.VMEM(held, bf16),
            pltpu.VMEM(held, bf16),
            pltpu.VMEM(held, bf16),
            pltpu.VMEM((every, HEAD), bf16),
            pltpu.VMEM((every, 2 * HEAD), bf16),
            pltpu.VMEM((2, BLOCK, every), f32),
            pltpu.VMEM((GROUPS, BLOCK, every), bf16),
            pltpu.VMEM((GROUPS, SIDE, PART, HEAD), bf16),
            pltpu.VMEM((SIDE - 1, GROUPS, PART, HEAD), bf16),
            pltpu.VMEM((2, GROUPS, BLOCK, HEAD), f32),
            pltpu.VMEM((SIDE, 2 * GROUPS, HEAD), f32),
            pltpu.VMEM((GROUPS, PART, HEAD), bf16),
            pltpu.VMEM((GROUPS, 4, TOK, HEAD), bf16),
            pltpu.SemaphoreType.DMA((4,)),
            pltpu.SemaphoreType.DMA((4,)),
            pltpu.SemaphoreType.DMA((4,)),
            pltpu.SemaphoreType.DMA((4,)),
            pltpu.SemaphoreType.DMA((2,)),
            pltpu.SemaphoreType.DMA,
            pltpu.SemaphoreType.DMA,
            pltpu.SemaphoreType.DMA,
            pltpu.SemaphoreType.DMA,
            pltpu.SemaphoreType.DMA((9,)),
        ],
        compiler_params=pltpu.CompilerParams(
            collective_id=0, has_side_effects=True, vmem_limit_bytes=40 * 2**20
        ),
    )(noise_levels, group_ids, queries, key_states, value_states, gate_table)


def solution(mesh):
    placed = (
        P(("group", "ctx"), None),
        P(("group", "ctx"), None),
        P(("group", "ctx"), None),
        P(),
        P(),
        P(),
    )
    return jax.shard_map(
        local, mesh=mesh, in_specs=placed, out_specs=P(("group", "ctx"), None), check_vma=False
    )
```

time: 214 us -> 73.8 us (0.34); the launches traced: 210 us -> 73.5 us
  Pallas kernels: 0 us -> 67.8 us
  blocking collectives: 65 us -> 0 us
  waiting for transfers between devices: 64.4 us -> 0 us
  starting transfers between devices: 24.4 us -> 0 us
  other arithmetic: 15.2 us -> 0 us
  matrix products: 14.4 us -> 0 us
  between operations: 13.6 us -> 0.02 us
  local copies, waits for them, and re-layouts: 13.3 us -> 5.72 us
    pallas_call x0 -> x1, Pallas kernels: none -> 67.8 us  [local(): pl.pallas_call(kernel, out_shape=jax.ShapeDtypeStruct((TOK, HEADS * HEAD)...]
    all_to_all x2 -> x0, blocking collectives: 65 us -> none  [the longest x1 39.8 us: local(): lax.all_to_all(doubled(key_states), 'ctx', split_axis=1, concat_axis=0, t...]
    all_to_all x2 -> x0, waiting for transfers between devices: 33 us -> none  [the longest x1 19.8 us: local(): lax.all_to_all(spread, 'ctx', split_axis=0, concat_axis=1, tiled=True)]
    all_gather x2 -> x0, waiting for transfers between devices: 29.5 us -> none  [the longest x1 28.4 us: local(): value_piece = lax.all_gather(value_heads, 'group', axis=0, tiled=True)]
    all_to_all x2 -> x0, starting transfers between devices: 20.6 us -> none  [the longest x1 15.8 us: local(): lax.all_to_all(spread, 'ctx', split_axis=0, concat_axis=1, tiled=True)]
    dot_general x2 -> x0, matrix products: 14.4 us -> none  [the longest x1 10.2 us: attend(): jnp.einsum('pqr,rpd->pqd', weights.astype(jnp.bfloat16), value_block, pre...]
    reduce_sum x5 -> x0, other arithmetic: 8.16 us -> none  [the longest x1 5.23 us: attend(): total = jnp.sum(weights, axis=-1)]
    ppermute x1 -> x0, starting transfers between devices: 3.74 us -> none  [shifted(): return lax.ppermute(block, axis, route)]
  transfers between devices with their start and end apart: 5 -> 0, of which waited for: 5 -> 0; matrix products, arithmetic and copies ran while one was open for 10% -> 0% of each run, Pallas kernels for 0% -> 0%
where the time goes in v1:
time: 73.8 us; the launch traced here: 73.5 us
  Pallas kernels  67.8 us (92%)
  local copies, waits for them, and re-layouts  5.72 us (8%)
    pallas_call x1, Pallas kernels, local(): pl.pallas_call(kernel, out_shape=jax.ShapeDtypeStruct((TOK, HEADS * HEAD)...  67.8 us
    unnamed x13, local copies, waits for them, and re-layouts  5.72 us

profile of v1, /device:TPU:1, one launch (start us, length us, event | category | flops | bytes accessed | tf_op | source)
XLA Modules:
  0.0 73.5 jit_solution(6031052330225598407)
XLA Ops:
  0.0 0.0 copy-start
  0.0 1.0 %copy-done = f32[32,4096]{1,0:T(8,128)S(1)} copy-done((f32[32,4096]{1,0:T(8,128)S(1)}, f32[32,4096]{1,0:T(8,128)}, u32[]{:S(2)}) %copy-start) | copy-done | bytes 524312
  1.0 0.0 copy-start.1
  1.0 0.9 %copy-done.1 = bf16[16,4096]{1,0:T(8,128)(2,1)S(1)} copy-done((bf16[16,4096]{1,0:T(8,128)(2,1)S(1)}, bf16[16,4096]{1,0:T(8,128)(2,1)}, u32[]{:S(2)}) %copy-start.1) | copy-done | bytes 131096
  1.9 0.0 copy-start.2
  1.9 0.9 %copy-done.2 = bf16[16,4096]{1,0:T(8,128)(2,1)S(1)} copy-done((bf16[16,4096]{1,0:T(8,128)(2,1)S(1)}, bf16[16,4096]{1,0:T(8,128)(2,1)}, u32[]{:S(2)}) %copy-start.2) | copy-done | bytes 131096
  2.9 0.0 copy-start.3
  2.9 0.9 %copy-done.3 = bf16[16,4096]{1,0:T(8,128)(2,1)S(1)} copy-done((bf16[16,4096]{1,0:T(8,128)(2,1)S(1)}, bf16[16,4096]{1,0:T(8,128)(2,1)}, u32[]{:S(2)}) %copy-start.3) | copy-done | bytes 131096
  3.8 0.0 copy-start.4
  3.8 0.7 copy-done.4
  4.4 0.0 copy-start.5
  4.4 0.7 copy-done.5
  5.1 67.8 %shard_map.64 = bf16[16,4096]{1,0:T(8,128)(2,1)S(1)} custom-call(s32[8]{0:T(128)S(1)} %copy-done.4, s32[8]{0:T(128)S(1)} %copy-done.5, bf16[16,4096]{1,0:T(8,128)(2,1)S(1)} %copy-done.1, bf16[16,4096]{1,0:T(8,128)(2,1)S(1)} %copy-done.2, bf16[16,4096]{1,0:T(8,128)(2,1)S(1)} %copy-done.3, f32[32,4096]{1,0:T(8,128)S(1)} %copy-done), custom_call_target="tpu_custom_call" | custom-call | tf_op jit(solution)/shard_map/pallas_call | solution.py:250
  72.9 0.7 copy.8
Async XLA Ops:
  0.0 1.0 %copy-start = (f32[32,4096]{1,0:T(8,128)S(1)}, f32[32,4096]{1,0:T(8,128)}, u32[]{:S(2)}) copy-start(f32[32,4096]{1,0:T(8,128)} %gate_ref.1) | copy-start | bytes 1572868
  1.0 0.9 %copy-start.1 = (bf16[16,4096]{1,0:T(8,128)(2,1)S(1)}, bf16[16,4096]{1,0:T(8,128)(2,1)}, u32[]{:S(2)}) copy-start(bf16[16,4096]{1,0:T(8,128)(2,1)} %q_ref.1) | copy-start | bytes 393220
  1.9 0.9 %copy-start.2 = (bf16[16,4096]{1,0:T(8,128)(2,1)S(1)}, bf16[16,4096]{1,0:T(8,128)(2,1)}, u32[]{:S(2)}) copy-start(bf16[16,4096]{1,0:T(8,128)(2,1)} %k_ref.1) | copy-start | bytes 393220
  2.9 0.9 %copy-start.3 = (bf16[16,4096]{1,0:T(8,128)(2,1)S(1)}, bf16[16,4096]{1,0:T(8,128)(2,1)}, u32[]{:S(2)}) copy-start(bf16[16,4096]{1,0:T(8,128)(2,1)} %v_ref.1) | copy-start | bytes 393220
  3.8 0.7 copy-start.4
  4.4 0.7 copy-start.5

commit v2 on v0

v2 whole, which is shorter than its diff:
```python
import functools
import math

import jax
import jax.numpy as jnp
from jax import lax
from jax.experimental import pallas as pl
from jax.experimental.pallas import tpu as pltpu
from jax.sharding import PartitionSpec as P

HEADS = 32
HEAD = 128
GROUPS = 8
TOK = 16
Z = 16
ZLO = 4
SQUARE = 4
PARTS = 4
FAR, NEAR = 0, 1
ROWS = SQUARE * TOK
BLOCK = PARTS * ROWS
SCALE = math.log2(math.e) / math.sqrt(HEAD)
MESH = pl.DeviceIdType.MESH


def kernel(
    levels_ref, ids_ref, q_ref, k_ref, v_ref, gate_ref, out_ref,
    q_in, k_in, v_in, gate, q_0, q_1, q_2, q_3, k_all, v_all, q_cat, k_cat, v_cat, scores, weights, summed,
    part_out, part_in, stats, merged, final,
    load_sem, kz_sem, qz_sem, vz_sem, kf_sem, qf_sem, vf_sem, o_sem, s_sem, f_sem, send_sem,
):
    group, ctx = lax.axis_index("group"), lax.axis_index("ctx")
    zlo, core = lax.div(group, 2), lax.rem(group, 2)
    x, y, zhi = lax.div(ctx, 16), lax.rem(lax.div(ctx, 4), 4), lax.rem(ctx, 4)
    z = zhi * ZLO + zlo

    def device(to_x, to_y, to_z, to_core):
        return (lax.rem(to_z, ZLO) * 2 + to_core, (to_x * 4 + to_y) * 4 + lax.div(to_z, ZLO))

    def column(head):
        return pl.ds(pl.multiple_of(head * HEAD, HEAD), HEAD)

    x_even, y_even = x + 1 - 2 * lax.rem(x, 2), y + 1 - 2 * lax.rem(y, 2)
    x_odd, y_odd = lax.rem(x + 3 + 2 * lax.rem(x, 2), 4), lax.rem(y + 3 + 2 * lax.rem(y, 2), 4)
    aligned = [device(x, y, z, core), device(x_even, y, z, core), device(x, y_even, z, core), device(x_even, y_even, z, core)]
    shifted = [device(x, y, z, core), device(x_odd, y, z, core), device(x, y_odd, z, core)]

    head = z * 2 + core
    loads = [
        pltpu.make_async_copy(k_ref, k_in, load_sem.at[0]),
        pltpu.make_async_copy(v_ref, v_in, load_sem.at[1]),
        pltpu.make_async_copy(q_ref, q_in, load_sem.at[2]),
        pltpu.make_async_copy(gate_ref.at[:, column(head)], gate, load_sem.at[3]),
    ]
    for load in loads:
        load.start()

    barrier = pltpu.get_barrier_semaphore()
    for peer in aligned[1:] + shifted[1:3]:
        pl.semaphore_signal(barrier, inc=1, device_id=peer, device_id_type=MESH)

    def greet(i, carry):
        target = device(x, y, lax.rem(z + lax.div(i, 2), Z), lax.rem(core + i, 2))
        pl.semaphore_signal(barrier, inc=1, device_id=target, device_id_type=MESH)
        return carry

    lax.fori_loop(1, 2 * Z, greet, 0)
    for load in loads:
        load.wait()
    pl.semaphore_wait(barrier, 2 * Z - 1 + 5)

    def wait_bytes(ref, sem):
        pltpu.make_async_copy(ref, ref, sem).wait()

    sent = []
    q_parts = (q_0, q_1, q_2, q_3)

    def distance(part, place):
        odd = lax.rem(place + part, 2)
        return place + (8 - 4 * odd if part < 2 else 4 * odd - 4)

    def spread(source, tile, arrived, number, part):
        def send(i, carry):
            place, other = lax.div(i, 2), lax.rem(i, 2)
            to_z, to_core = lax.rem(z + Z - distance(part, place), Z), lax.rem(core + other, 2)
            pltpu.make_async_remote_copy(
                src_ref=source.at[:, column(to_z * 2 + to_core)],
                dst_ref=tile(place),
                send_sem=send_sem.at[number],
                recv_sem=arrived,
                device_id=device(x, y, to_z, to_core),
                device_id_type=MESH,
            ).start()
            return carry

        if part == PARTS - 1:
            pltpu.make_async_copy(source.at[:, column(head)], tile(0), arrived).start()
            lax.fori_loop(1, 8, send, 0)
        else:
            lax.fori_loop(0, 8, send, 0)

    for part in range(PARTS):
        spread(k_in, lambda place: k_all.at[0, part, place, core], kz_sem.at[part // 2], 0, part)
    for part in range(PARTS):
        spread(v_in, lambda place: v_all.at[0, part, place, core], vz_sem.at[part // 2], 1, part)
    for part in range(PARTS):
        spread(q_in, lambda place: q_parts[part].at[0, place, core], qz_sem.at[part], 2, part)
    sent += [(source.at[:, pl.ds(0, (2 * Z - 1) * HEAD)], number) for number, source in enumerate((k_in, v_in, q_in))]

    halves = (pl.ds(0, 2), pl.ds(2, 2))
    others = pl.ds(1, SQUARE - 1)

    def pass_on(source, target_ref, target, number, receive):
        pltpu.make_async_remote_copy(
            src_ref=source,
            dst_ref=target_ref,
            send_sem=send_sem.at[number],
            recv_sem=receive,
            device_id=target,
            device_id_type=MESH,
        ).start()

    def pass_near(buffer, arrived, number, receive):
        for half, span in enumerate(halves):
            wait_bytes(buffer.at[0, span], arrived.at[half])
            for step in (1, 2):
                early = half == step - 1
                pass_on(
                    buffer.at[0, span], buffer.at[step, span], shifted[step], number, receive.at[half if early else 2]
                )

    def pass_across(buffer, number, receive):
        for half, span in enumerate(halves):
            wait_bytes(buffer.at[half + 1, span], receive.at[half])
            pass_on(buffer.at[half + 1, span], buffer.at[3, span], shifted[2 - half], number, receive.at[2])

    def pass_queries(part):
        queries = q_parts[part]
        wait_bytes(queries.at[0], qz_sem.at[part])
        for step in range(1, SQUARE):
            pass_on(queries.at[0], queries.at[step], aligned[step], 5, qf_sem.at[part])

    pass_near(k_all, kz_sem, 3, kf_sem)
    pass_across(k_all, 3, kf_sem)
    pass_near(v_all, vz_sem, 4, vf_sem)
    pass_queries(0)
    pass_across(v_all, 4, vf_sem)
    pass_queries(1)
    pass_queries(2)

    def holder(rank):
        found = jnp.int32(0)
        for g in range(GROUPS):
            found = found + jnp.where(ids_ref[g] == rank, jnp.int32(g), jnp.int32(0))
        return found

    ranked = [holder(rank) for rank in range(GROUPS)]
    places = [(lax.rem(lax.div(g, 2) - zlo + ZLO, ZLO), lax.rem(g, 2)) for g in ranked]

    wait_bytes(k_all.at[pl.ds(1, 2)], kf_sem.at[2])
    for rank, (near, side) in enumerate(places):
        k_cat[pl.ds(rank * BLOCK, BLOCK), :] = k_all[:, :, near, side].reshape(BLOCK, HEAD)
    v_cat[:, HEAD:] = jnp.ones((GROUPS * BLOCK, HEAD), jnp.bfloat16)
    pass_queries(3)
    wait_bytes(v_all.at[pl.ds(1, 2)], vf_sem.at[2])
    for rank, (near, side) in enumerate(places):
        v_cat[pl.ds(rank * BLOCK, BLOCK), :HEAD] = v_all[:, :, near, side].reshape(BLOCK, HEAD)
    sent += [(k_all.at[others], 3), (v_all.at[others], 4), (k_all.at[others], 5)]

    rows = lax.broadcasted_iota(jnp.int32, (ROWS, HEAD), 0)
    lanes = lax.broadcasted_iota(jnp.int32, (ROWS, HEAD), 1)
    diagonal = rows == lanes

    def attend(part):
        wait_bytes(q_parts[part].at[others], qf_sem.at[part])
        for rank, (near, side) in enumerate(places):
            q_cat[pl.ds(rank * ROWS, ROWS), :] = q_parts[part][:, near, side].reshape(ROWS, HEAD)
        for block in range(GROUPS):
            below = pl.ds(block * ROWS, (GROUPS - block) * ROWS)
            span = pl.ds(block * BLOCK, BLOCK)
            scores[below, span] = lax.dot_general(
                q_cat[below, :], k_cat[span, :], (((1,), (1,)), ((), ())), preferred_element_type=jnp.float32
            )
        peaks = []
        for rank in range(GROUPS):
            own = pl.ds(rank * ROWS, ROWS)
            strips = [scores[own, pl.ds(i * HEAD, HEAD)] for i in range((rank + 1) * BLOCK // HEAD)]
            peak = jnp.max(functools.reduce(jnp.maximum, strips), axis=1, keepdims=True)
            peaks.append(peak)
            for block in range(rank + 1):
                span = pl.ds(block * BLOCK, BLOCK)
                weights[own, span] = jnp.exp2((scores[own, span] - peak) * SCALE).astype(jnp.bfloat16)
        for block in range(GROUPS):
            below = pl.ds(block * ROWS, (GROUPS - block) * ROWS)
            span = pl.ds(block * BLOCK, BLOCK)
            product = jnp.dot(weights[below, span], v_cat[span, :], preferred_element_type=jnp.float32)
            if block == 0:
                summed[below, :] = product
            else:
                summed[below, :] += product
        for rank in range(GROUPS):
            own = pl.ds(rank * ROWS, ROWS)
            total = summed[own, HEAD:]
            part_out[part, :, rank] = (summed[own, :HEAD] / total).astype(jnp.bfloat16).reshape(SQUARE, TOK, HEAD)
            logs = peaks[rank] * SCALE + jnp.log2(total)
            stats[part, 0, pl.ds(rank, 1), :] = jnp.sum(jnp.where(diagonal, logs, 0.0), axis=0, keepdims=True)
        for step in range(1, SQUARE):
            pltpu.make_async_remote_copy(
                src_ref=part_out.at[part, step],
                dst_ref=part_in.at[part, step - 1],
                send_sem=send_sem.at[6],
                recv_sem=o_sem.at[part],
                device_id=aligned[step],
                device_id_type=MESH,
            ).start()
            pltpu.make_async_remote_copy(
                src_ref=stats.at[part, 0],
                dst_ref=stats.at[part, step],
                send_sem=send_sem.at[7],
                recv_sem=s_sem.at[part],
                device_id=aligned[step],
                device_id_type=MESH,
            ).start()

    own_rows = lax.broadcasted_iota(jnp.int32, (TOK, HEAD), 0)
    own_lanes = lax.broadcasted_iota(jnp.int32, (TOK, HEAD), 1)

    def merge(part):
        wait_bytes(part_in.at[part], o_sem.at[part])
        wait_bytes(stats.at[part, others], s_sem.at[part])
        for rank in range(GROUPS):
            logs = []
            for step in range(SQUARE):
                line = stats[part, step, pl.ds(rank, 1), :]
                picked = jnp.where(own_lanes == own_rows + step * TOK, line, 0.0)
                logs.append(jnp.sum(picked, axis=1, keepdims=True))
            top = functools.reduce(jnp.maximum, logs)
            shares = [jnp.exp2(log - top) for log in logs]
            whole = functools.reduce(jnp.add, shares)
            value = part_out[part, 0, rank].astype(jnp.float32) * (shares[0] / whole)
            for step in range(1, SQUARE):
                value = value + part_in[part, step - 1, rank].astype(jnp.float32) * (shares[step] / whole)
            merged[part, rank] = value.astype(jnp.bfloat16)
        for g in range(GROUPS):
            row = gate[pl.ds(levels_ref[g], 1), :]
            done = merged[part, ids_ref[g]].astype(jnp.float32) * row
            final[part, g] = done.astype(jnp.bfloat16)

        def send(i, carry):
            place, side = lax.div(i, 2), lax.rem(i, 2)
            from_z = lax.rem(z + Z + distance(part, place), Z)
            from_group = lax.rem(from_z, ZLO) * 2 + side
            to_group = lax.rem(from_group + 1, GROUPS)
            to_z, to_core = lax.div(from_z, ZLO) * ZLO + lax.div(to_group, 2), lax.rem(to_group, 2)
            away = jnp.logical_or(to_z != z, to_core != core)

            @pl.when(away)
            def _():
                pltpu.make_async_remote_copy(
                    src_ref=final.at[part, from_group],
                    dst_ref=out_ref.at[:, column(head)],
                    send_sem=send_sem.at[8],
                    recv_sem=f_sem,
                    device_id=device(x, y, to_z, to_core),
                    device_id_type=MESH,
                ).start()

            @pl.when(jnp.logical_not(away))
            def _():
                pltpu.make_async_copy(final.at[part, from_group], out_ref.at[:, column(head)], f_sem).start()

            return carry

        lax.fori_loop(0, 8, send, 0)

    for part in range(PARTS):
        attend(part)
    sent += [(part_in, 6), (stats.at[:, others], 7), (k_in.at[:, pl.ds(0, (2 * Z - 1) * HEAD)], 8)]
    for part in range(PARTS):
        merge(part)
    for ref, number in sent:
        wait_bytes(ref, send_sem.at[number])
    wait_bytes(out_ref, f_sem)


def local(queries, key_states, value_states, gate_table, noise_levels, group_ids):
    bf16, f32 = jnp.bfloat16, jnp.float32
    held = (SQUARE, PARTS, ZLO, 2, TOK, HEAD)
    every = GROUPS * BLOCK
    return pl.pallas_call(
        kernel,
        out_shape=jax.ShapeDtypeStruct((TOK, HEADS * HEAD), bf16),
        in_specs=[pl.BlockSpec(memory_space=pltpu.SMEM)] * 2 + [pl.BlockSpec(memory_space=pl.ANY)] * 4,
        out_specs=pl.BlockSpec(memory_space=pltpu.VMEM),
        scratch_shapes=[
            pltpu.VMEM((TOK, HEADS * HEAD), bf16),
            pltpu.VMEM((TOK, HEADS * HEAD), bf16),
            pltpu.VMEM((TOK, HEADS * HEAD), bf16),
            pltpu.VMEM((32, HEAD), f32),
            *[pltpu.VMEM((SQUARE, ZLO, 2, TOK, HEAD), bf16)] * PARTS,
            pltpu.VMEM(held, bf16),
            pltpu.VMEM(held, bf16),
            pltpu.VMEM((GROUPS * ROWS, HEAD), bf16),
            pltpu.VMEM((every, HEAD), bf16),
            pltpu.VMEM((every, 2 * HEAD), bf16),
            pltpu.VMEM((GROUPS * ROWS, every), f32),
            pltpu.VMEM((GROUPS * ROWS, every), bf16),
            pltpu.VMEM((GROUPS * ROWS, 2 * HEAD), f32),
            pltpu.VMEM((PARTS, SQUARE, GROUPS, TOK, HEAD), bf16),
            pltpu.VMEM((PARTS, SQUARE - 1, GROUPS, TOK, HEAD), bf16),
            pltpu.VMEM((PARTS, SQUARE, GROUPS, HEAD), f32),
            pltpu.VMEM((PARTS, GROUPS, TOK, HEAD), bf16),
            pltpu.VMEM((PARTS, GROUPS, TOK, HEAD), bf16),
            pltpu.SemaphoreType.DMA((4,)),
            pltpu.SemaphoreType.DMA((2,)),
            pltpu.SemaphoreType.DMA((PARTS,)),
            pltpu.SemaphoreType.DMA((2,)),
            pltpu.SemaphoreType.DMA((3,)),
            pltpu.SemaphoreType.DMA((PARTS,)),
            pltpu.SemaphoreType.DMA((3,)),
            pltpu.SemaphoreType.DMA((PARTS,)),
            pltpu.SemaphoreType.DMA((PARTS,)),
            pltpu.SemaphoreType.DMA,
            pltpu.SemaphoreType.DMA((9,)),
        ],
        compiler_params=pltpu.CompilerParams(
            collective_id=0, has_side_effects=True, vmem_limit_bytes=56 * 2**20
        ),
    )(noise_levels, group_ids, queries, key_states, value_states, gate_table)


def solution(mesh):
    placed = (
        P(("group", "ctx"), None),
        P(("group", "ctx"), None),
        P(("group", "ctx"), None),
        P(),
        P(),
        P(),
    )
    return jax.shard_map(
        local, mesh=mesh, in_specs=placed, out_specs=P(("group", "ctx"), None), check_vma=False
    )
```

time: 214 us -> 62 us (0.29); the launches traced: 210 us -> 61.8 us
  blocking collectives: 65 us -> 0 us
  waiting for transfers between devices: 64.4 us -> 0 us
  Pallas kernels: 0 us -> 60.3 us
  starting transfers between devices: 24.4 us -> 0 us
  other arithmetic: 15.2 us -> 0 us
  matrix products: 14.4 us -> 0 us
  between operations: 13.6 us -> 0.01 us
  local copies, waits for them, and re-layouts: 13.3 us -> 1.57 us
    all_to_all x2 -> x0, blocking collectives: 65 us -> none  [the longest x1 39.8 us: local(): lax.all_to_all(doubled(key_states), 'ctx', split_axis=1, concat_axis=0, t...]
    pallas_call x0 -> x1, Pallas kernels: none -> 60.3 us  [local(): pl.pallas_call(kernel, out_shape=jax.ShapeDtypeStruct((TOK, HEADS * HEAD)...]
    all_to_all x2 -> x0, waiting for transfers between devices: 33 us -> none  [the longest x1 19.8 us: local(): lax.all_to_all(spread, 'ctx', split_axis=0, concat_axis=1, tiled=True)]
    all_gather x2 -> x0, waiting for transfers between devices: 29.5 us -> none  [the longest x1 28.4 us: local(): value_piece = lax.all_gather(value_heads, 'group', axis=0, tiled=True)]
    all_to_all x2 -> x0, starting transfers between devices: 20.6 us -> none  [the longest x1 15.8 us: local(): lax.all_to_all(spread, 'ctx', split_axis=0, concat_axis=1, tiled=True)]
    dot_general x2 -> x0, matrix products: 14.4 us -> none  [the longest x1 10.2 us: attend(): jnp.einsum('pqr,rpd->pqd', weights.astype(jnp.bfloat16), value_block, pre...]
    reduce_sum x5 -> x0, other arithmetic: 8.16 us -> none  [the longest x1 5.23 us: attend(): total = jnp.sum(weights, axis=-1)]
    unnamed x12 -> x1, local copies, waits for them, and re-layouts: 8.27 us -> 1.57 us
  transfers between devices with their start and end apart: 5 -> 0, of which waited for: 5 -> 0; matrix products, arithmetic and copies ran while one was open for 10% -> 0% of each run, Pallas kernels for 0% -> 0%
where the time goes in v2:
time: 62 us; the launch traced here: 61.8 us
  Pallas kernels  60.3 us (97%)
  local copies, waits for them, and re-layouts  1.57 us (3%)
    pallas_call x1, Pallas kernels, local(): pl.pallas_call(kernel, out_shape=jax.ShapeDtypeStruct((TOK, HEADS * HEAD)...  60.3 us
    unnamed x1, local copies, waits for them, and re-layouts  1.57 us

profile of v2, /device:TPU:1, one launch (start us, length us, event | category | flops | bytes accessed | tf_op | source)
XLA Modules:
  0.0 61.8 jit_solution(7150151301339644091)
XLA Ops:
  0.0 60.3 %shard_map.64 = bf16[16,4096]{1,0:T(8,128)(2,1)} custom-call(s32[8]{0:T(128)} %levels_ref.1, s32[8]{0:T(128)} %ids_ref.1, bf16[16,4096]{1,0:T(8,128)(2,1)} %q_ref.1, bf16[16,4096]{1,0:T(8,128)(2,1)} %k_ref.1, bf16[16,4096]{1,0:T(8,128)(2,1)} %v_ref.1, f32[32,4096]{1,0:T(8,128)} %gate_ref.1), custom_call_target="tpu_custom_call" | custom-call | tf_op jit(solution)/shard_map/pallas_call | solution.py:290
  60.3 1.6 %copy.8 = bf16[16,4096]{1,0:T(8,128)(2,1)} copy(bf16[16,4096]{1,0:T(8,128)(2,1)} %shard_map.64) | data formatting | bytes 262144

commit v3 on v2

--- a/solution.py
+++ b/solution.py
@@ -16,7 +16,6 @@
 ZLO = 4
 SQUARE = 4
 PARTS = 4
-FAR, NEAR = 0, 1
 ROWS = SQUARE * TOK
 BLOCK = PARTS * ROWS
 SCALE = math.log2(math.e) / math.sqrt(HEAD)
@@ -40,10 +39,15 @@
     def column(head):
         return pl.ds(pl.multiple_of(head * HEAD, HEAD), HEAD)
 
-    x_even, y_even = x + 1 - 2 * lax.rem(x, 2), y + 1 - 2 * lax.rem(y, 2)
-    x_odd, y_odd = lax.rem(x + 3 + 2 * lax.rem(x, 2), 4), lax.rem(y + 3 + 2 * lax.rem(y, 2), 4)
-    aligned = [device(x, y, z, core), device(x_even, y, z, core), device(x, y_even, z, core), device(x_even, y_even, z, core)]
-    shifted = [device(x, y, z, core), device(x_odd, y, z, core), device(x, y_odd, z, core)]
+    def square(shift):
+        def partner(position):
+            moved = lax.rem(position + shift, 4)
+            return lax.rem(moved + 1 - 2 * lax.rem(moved, 2) + 4 - shift, 4)
+
+        to_x, to_y = partner(x), partner(y)
+        return [device(to_x, y, z, core), device(x, to_y, z, core), device(to_x, to_y, z, core)]
+
+    key_square, query_square = square(1 - core), square(core)
 
     head = z * 2 + core
     loads = [
@@ -56,7 +60,7 @@
         load.start()
 
     barrier = pltpu.get_barrier_semaphore()
-    for peer in aligned[1:] + shifted[1:3]:
+    for peer in query_square + key_square:
         pl.semaphore_signal(barrier, inc=1, device_id=peer, device_id_type=MESH)
 
     def greet(i, carry):
@@ -67,7 +71,7 @@
     lax.fori_loop(1, 2 * Z, greet, 0)
     for load in loads:
         load.wait()
-    pl.semaphore_wait(barrier, 2 * Z - 1 + 5)
+    pl.semaphore_wait(barrier, 2 * Z - 1 + 2 * (SQUARE - 1))
 
     def wait_bytes(ref, sem):
         pltpu.make_async_copy(ref, ref, sem).wait()
@@ -99,15 +103,20 @@
         else:
             lax.fori_loop(0, 8, send, 0)
 
-    for part in range(PARTS):
-        spread(k_in, lambda place: k_all.at[0, part, place, core], kz_sem.at[part // 2], 0, part)
-    for part in range(PARTS):
-        spread(v_in, lambda place: v_all.at[0, part, place, core], vz_sem.at[part // 2], 1, part)
-    for part in range(PARTS):
-        spread(q_in, lambda place: q_parts[part].at[0, place, core], qz_sem.at[part], 2, part)
+    for part in (1, 0):
+        spread(k_in, lambda place: k_all.at[0, part, place, core], kz_sem.at[part], 0, part)
+    for part in (3, 2):
+        spread(k_in, lambda place: k_all.at[0, part, place, core], kz_sem.at[part], 0, part)
+    for part in (1, 0):
+        spread(v_in, lambda place: v_all.at[0, part, place, core], vz_sem.at[part], 1, part)
+    for part in (3, 2):
+        spread(v_in, lambda place: v_all.at[0, part, place, core], vz_sem.at[part], 1, part)
+    def spread_queries(parts):
+        for part in parts:
+            spread(q_in, lambda place: q_parts[part].at[0, place, core], qz_sem.at[part], 2, part)
+
     sent += [(source.at[:, pl.ds(0, (2 * Z - 1) * HEAD)], number) for number, source in enumerate((k_in, v_in, q_in))]
 
-    halves = (pl.ds(0, 2), pl.ds(2, 2))
     others = pl.ds(1, SQUARE - 1)
 
     def pass_on(source, target_ref, target, number, receive):
@@ -120,33 +129,29 @@
             device_id_type=MESH,
         ).start()
 
-    def pass_near(buffer, arrived, number, receive):
-        for half, span in enumerate(halves):
-            wait_bytes(buffer.at[0, span], arrived.at[half])
-            for step in (1, 2):
-                early = half == step - 1
-                pass_on(
-                    buffer.at[0, span], buffer.at[step, span], shifted[step], number, receive.at[half if early else 2]
-                )
-
-    def pass_across(buffer, number, receive):
-        for half, span in enumerate(halves):
-            wait_bytes(buffer.at[half + 1, span], receive.at[half])
-            pass_on(buffer.at[half + 1, span], buffer.at[3, span], shifted[2 - half], number, receive.at[2])
+    def pass_part(buffer, part, arrived, number, receive):
+        wait_bytes(buffer.at[0, part], arrived.at[part])
+        for step in range(1, SQUARE):
+            pass_on(buffer.at[0, part], buffer.at[step, part], key_square[step - 1], number, receive)
 
     def pass_queries(part):
         queries = q_parts[part]
         wait_bytes(queries.at[0], qz_sem.at[part])
         for step in range(1, SQUARE):
-            pass_on(queries.at[0], queries.at[step], aligned[step], 5, qf_sem.at[part])
-
-    pass_near(k_all, kz_sem, 3, kf_sem)
-    pass_across(k_all, 3, kf_sem)
-    pass_near(v_all, vz_sem, 4, vf_sem)
-    pass_queries(0)
-    pass_across(v_all, 4, vf_sem)
-    pass_queries(1)
-    pass_queries(2)
+            pass_on(queries.at[0], queries.at[step], query_square[step - 1], 5, qf_sem.at[part])
+
+    for part in (1, 0):
+        pass_part(k_all, part, kz_sem, 3, kf_sem)
+    for part in (3, 2):
+        pass_part(k_all, part, kz_sem, 3, kf_sem)
+    spread_queries((0, 1))
+    for part in (1, 0):
+        pass_part(v_all, part, vz_sem, 4, vf_sem)
+    for part in (3, 2):
+        pass_part(v_all, part, vz_sem, 4, vf_sem)
+    spread_queries((2, 3))
+    for part in range(PARTS - 1):
+        pass_queries(part)
 
     def holder(rank):
         found = jnp.int32(0)
@@ -157,21 +162,17 @@
     ranked = [holder(rank) for rank in range(GROUPS)]
     places = [(lax.rem(lax.div(g, 2) - zlo + ZLO, ZLO), lax.rem(g, 2)) for g in ranked]
 
-    wait_bytes(k_all.at[pl.ds(1, 2)], kf_sem.at[2])
+    wait_bytes(k_all.at[others], kf_sem)
     for rank, (near, side) in enumerate(places):
         k_cat[pl.ds(rank * BLOCK, BLOCK), :] = k_all[:, :, near, side].reshape(BLOCK, HEAD)
-    v_cat[:, HEAD:] = jnp.ones((GROUPS * BLOCK, HEAD), jnp.bfloat16)
-    pass_queries(3)
-    wait_bytes(v_all.at[pl.ds(1, 2)], vf_sem.at[2])
-    for rank, (near, side) in enumerate(places):
-        v_cat[pl.ds(rank * BLOCK, BLOCK), :HEAD] = v_all[:, :, near, side].reshape(BLOCK, HEAD)
+    pass_queries(PARTS - 1)
     sent += [(k_all.at[others], 3), (v_all.at[others], 4), (k_all.at[others], 5)]
 
     rows = lax.broadcasted_iota(jnp.int32, (ROWS, HEAD), 0)
     lanes = lax.broadcasted_iota(jnp.int32, (ROWS, HEAD), 1)
     diagonal = rows == lanes
 
-    def attend(part):
+    def score(part):
         wait_bytes(q_parts[part].at[others], qf_sem.at[part])
         for rank, (near, side) in enumerate(places):
             q_cat[pl.ds(rank * ROWS, ROWS), :] = q_parts[part][:, near, side].reshape(ROWS, HEAD)
@@ -190,6 +191,9 @@
             for block in range(rank + 1):
                 span = pl.ds(block * BLOCK, BLOCK)
                 weights[own, span] = jnp.exp2((scores[own, span] - peak) * SCALE).astype(jnp.bfloat16)
+        return peaks
+
+    def attend(part, peaks):
         for block in range(GROUPS):
             below = pl.ds(block * ROWS, (GROUPS - block) * ROWS)
             span = pl.ds(block * BLOCK, BLOCK)
@@ -210,7 +214,7 @@
                 dst_ref=part_in.at[part, step - 1],
                 send_sem=send_sem.at[6],
                 recv_sem=o_sem.at[part],
-                device_id=aligned[step],
+                device_id=query_square[step - 1],
                 device_id_type=MESH,
             ).start()
             pltpu.make_async_remote_copy(
@@ -218,7 +222,7 @@
                 dst_ref=stats.at[part, step],
                 send_sem=send_sem.at[7],
                 recv_sem=s_sem.at[part],
-                device_id=aligned[step],
+                device_id=query_square[step - 1],
                 device_id_type=MESH,
             ).start()
 
@@ -246,6 +250,7 @@
             done = merged[part, ids_ref[g]].astype(jnp.float32) * row
             final[part, g] = done.astype(jnp.bfloat16)
 
+    def give(part, lower):
         def send(i, carry):
             place, side = lax.div(i, 2), lax.rem(i, 2)
             from_z = lax.rem(z + Z + distance(part, place), Z)
@@ -253,8 +258,9 @@
             to_group = lax.rem(from_group + 1, GROUPS)
             to_z, to_core = lax.div(from_z, ZLO) * ZLO + lax.div(to_group, 2), lax.rem(to_group, 2)
             away = jnp.logical_or(to_z != z, to_core != core)
-
-            @pl.when(away)
+            now = to_z < Z // 2 if lower else to_z >= Z // 2
+
+            @pl.when(jnp.logical_and(now, away))
             def _():
                 pltpu.make_async_remote_copy(
                     src_ref=final.at[part, from_group],
@@ -265,7 +271,7 @@
                     device_id_type=MESH,
                 ).start()
 
-            @pl.when(jnp.logical_not(away))
+            @pl.when(jnp.logical_and(now, jnp.logical_not(away)))
             def _():
                 pltpu.make_async_copy(final.at[part, from_group], out_ref.at[:, column(head)], f_sem).start()
 
@@ -273,11 +279,23 @@
 
         lax.fori_loop(0, 8, send, 0)
 
+    peaks = score(0)
+    v_cat[:, HEAD:] = jnp.ones((GROUPS * BLOCK, HEAD), jnp.bfloat16)
+    wait_bytes(v_all.at[others], vf_sem)
+    for rank, (near, side) in enumerate(places):
+        v_cat[pl.ds(rank * BLOCK, BLOCK), :HEAD] = v_all[:, :, near, side].reshape(BLOCK, HEAD)
+    attend(0, peaks)
+    attend(1, score(1))
+    attend(2, score(2))
+    merge(0)
+    give(0, True)
+    attend(3, score(3))
+    sent += [(part_in, 6), (stats.at[:, others], 7), (k_in.at[:, pl.ds(0, (2 * Z - 1) * HEAD)], 8)]
+    for part in range(1, PARTS):
+        merge(part)
+        give(part, True)
     for part in range(PARTS):
-        attend(part)
-    sent += [(part_in, 6), (stats.at[:, others], 7), (k_in.at[:, pl.ds(0, (2 * Z - 1) * HEAD)], 8)]
-    for part in range(PARTS):
-        merge(part)
+        give(part, False)
     for ref, number in sent:
         wait_bytes(ref, send_sem.at[number])
     wait_bytes(out_ref, f_sem)
@@ -312,12 +330,12 @@
             pltpu.VMEM((PARTS, GROUPS, TOK, HEAD), bf16),
             pltpu.VMEM((PARTS, GROUPS, TOK, HEAD), bf16),
             pltpu.SemaphoreType.DMA((4,)),
-            pltpu.SemaphoreType.DMA((2,)),
-            pltpu.SemaphoreType.DMA((PARTS,)),
-            pltpu.SemaphoreType.DMA((2,)),
-            pltpu.SemaphoreType.DMA((3,)),
-            pltpu.SemaphoreType.DMA((PARTS,)),
-            pltpu.SemaphoreType.DMA((3,)),
+            pltpu.SemaphoreType.DMA((PARTS,)),
+            pltpu.SemaphoreType.DMA((PARTS,)),
+            pltpu.SemaphoreType.DMA((PARTS,)),
+            pltpu.SemaphoreType.DMA,
+            pltpu.SemaphoreType.DMA((PARTS,)),
+            pltpu.SemaphoreType.DMA,
             pltpu.SemaphoreType.DMA((PARTS,)),
             pltpu.SemaphoreType.DMA((PARTS,)),
             pltpu.SemaphoreType.DMA,

time: 62 us -> 60.8 us (0.981)
  Pallas kernels: 60.3 us -> 59.1 us
    pallas_call x1, Pallas kernels: 60.3 us -> 59.1 us  [local(): pl.pallas_call(kernel, out_shape=jax.ShapeDtypeStruct((TOK, HEADS * HEAD)...]
where the time goes in v3:
time: 60.8 us; the launch traced here: 60.7 us
  Pallas kernels  59.1 us (97%)
  local copies, waits for them, and re-layouts  1.57 us (3%)
    pallas_call x1, Pallas kernels, local(): pl.pallas_call(kernel, out_shape=jax.ShapeDtypeStruct((TOK, HEADS * HEAD)...  59.1 us
    unnamed x1, local copies, waits for them, and re-layouts  1.57 us

profile of v3, /device:TPU:1, one launch (start us, length us, event | category | flops | bytes accessed | tf_op | source)
XLA Modules:
  0.0 60.7 jit_solution(16081661164251815186)
XLA Ops:
  0.0 59.1 %shard_map.64 = bf16[16,4096]{1,0:T(8,128)(2,1)} custom-call(s32[8]{0:T(128)} %levels_ref.1, s32[8]{0:T(128)} %ids_ref.1, bf16[16,4096]{1,0:T(8,128)(2,1)} %q_ref.1, bf16[16,4096]{1,0:T(8,128)(2,1)} %k_ref.1, bf16[16,4096]{1,0:T(8,128)(2,1)} %v_ref.1, f32[32,4096]{1,0:T(8,128)} %gate_ref.1), custom_call_target="tpu_custom_call" | custom-call | tf_op jit(solution)/shard_map/pallas_call | solution.py:308
  59.1 1.6 %copy.8 = bf16[16,4096]{1,0:T(8,128)(2,1)} copy(bf16[16,4096]{1,0:T(8,128)(2,1)} %shard_map.64) | data formatting | bytes 262144

commit v4 on v3

--- a/solution.py
+++ b/solution.py
@@ -18,6 +18,7 @@
 PARTS = 4
 ROWS = SQUARE * TOK
 BLOCK = PARTS * ROWS
+ACROSS_FIRST = (3, 1, 2)
 SCALE = math.log2(math.e) / math.sqrt(HEAD)
 MESH = pl.DeviceIdType.MESH
 
@@ -80,28 +81,24 @@
     q_parts = (q_0, q_1, q_2, q_3)
 
     def distance(part, place):
-        odd = lax.rem(place + part, 2)
+        odd = (place + part) % 2
         return place + (8 - 4 * odd if part < 2 else 4 * odd - 4)
 
     def spread(source, tile, arrived, number, part):
-        def send(i, carry):
-            place, other = lax.div(i, 2), lax.rem(i, 2)
-            to_z, to_core = lax.rem(z + Z - distance(part, place), Z), lax.rem(core + other, 2)
-            pltpu.make_async_remote_copy(
-                src_ref=source.at[:, column(to_z * 2 + to_core)],
-                dst_ref=tile(place),
-                send_sem=send_sem.at[number],
-                recv_sem=arrived,
-                device_id=device(x, y, to_z, to_core),
-                device_id_type=MESH,
-            ).start()
-            return carry
-
-        if part == PARTS - 1:
-            pltpu.make_async_copy(source.at[:, column(head)], tile(0), arrived).start()
-            lax.fori_loop(1, 8, send, 0)
-        else:
-            lax.fori_loop(0, 8, send, 0)
+        for place in range(ZLO):
+            to_z = lax.rem(z + Z - distance(part, place), Z)
+            for to_core in (core, 1 - core):
+                if distance(part, place) == 0 and to_core is core:
+                    pltpu.make_async_copy(source.at[:, column(head)], tile(place), arrived).start()
+                    continue
+                pltpu.make_async_remote_copy(
+                    src_ref=source.at[:, column(to_z * 2 + to_core)],
+                    dst_ref=tile(place),
+                    send_sem=send_sem.at[number],
+                    recv_sem=arrived,
+                    device_id=device(x, y, to_z, to_core),
+                    device_id_type=MESH,
+                ).start()
 
     for part in (1, 0):
         spread(k_in, lambda place: k_all.at[0, part, place, core], kz_sem.at[part], 0, part)
@@ -111,6 +108,7 @@
         spread(v_in, lambda place: v_all.at[0, part, place, core], vz_sem.at[part], 1, part)
     for part in (3, 2):
         spread(v_in, lambda place: v_all.at[0, part, place, core], vz_sem.at[part], 1, part)
+
     def spread_queries(parts):
         for part in parts:
             spread(q_in, lambda place: q_parts[part].at[0, place, core], qz_sem.at[part], 2, part)
@@ -131,13 +129,13 @@
 
     def pass_part(buffer, part, arrived, number, receive):
         wait_bytes(buffer.at[0, part], arrived.at[part])
-        for step in range(1, SQUARE):
+        for step in ACROSS_FIRST:
             pass_on(buffer.at[0, part], buffer.at[step, part], key_square[step - 1], number, receive)
 
     def pass_queries(part):
         queries = q_parts[part]
         wait_bytes(queries.at[0], qz_sem.at[part])
-        for step in range(1, SQUARE):
+        for step in ACROSS_FIRST:
             pass_on(queries.at[0], queries.at[step], query_square[step - 1], 5, qf_sem.at[part])
 
     for part in (1, 0):
@@ -208,7 +206,7 @@
             part_out[part, :, rank] = (summed[own, :HEAD] / total).astype(jnp.bfloat16).reshape(SQUARE, TOK, HEAD)
             logs = peaks[rank] * SCALE + jnp.log2(total)
             stats[part, 0, pl.ds(rank, 1), :] = jnp.sum(jnp.where(diagonal, logs, 0.0), axis=0, keepdims=True)
-        for step in range(1, SQUARE):
+        for step in ACROSS_FIRST:
             pltpu.make_async_remote_copy(
                 src_ref=part_out.at[part, step],
                 dst_ref=part_in.at[part, step - 1],
@@ -250,34 +248,33 @@
             done = merged[part, ids_ref[g]].astype(jnp.float32) * row
             final[part, g] = done.astype(jnp.bfloat16)
 
-    def give(part, lower):
-        def send(i, carry):
-            place, side = lax.div(i, 2), lax.rem(i, 2)
+    def give(part):
+        for place in range(ZLO):
             from_z = lax.rem(z + Z + distance(part, place), Z)
-            from_group = lax.rem(from_z, ZLO) * 2 + side
-            to_group = lax.rem(from_group + 1, GROUPS)
-            to_z, to_core = lax.div(from_z, ZLO) * ZLO + lax.div(to_group, 2), lax.rem(to_group, 2)
-            away = jnp.logical_or(to_z != z, to_core != core)
-            now = to_z < Z // 2 if lower else to_z >= Z // 2
-
-            @pl.when(jnp.logical_and(now, away))
-            def _():
-                pltpu.make_async_remote_copy(
-                    src_ref=final.at[part, from_group],
-                    dst_ref=out_ref.at[:, column(head)],
-                    send_sem=send_sem.at[8],
-                    recv_sem=f_sem,
-                    device_id=device(x, y, to_z, to_core),
-                    device_id_type=MESH,
-                ).start()
-
-            @pl.when(jnp.logical_and(now, jnp.logical_not(away)))
-            def _():
-                pltpu.make_async_copy(final.at[part, from_group], out_ref.at[:, column(head)], f_sem).start()
-
-            return carry
-
-        lax.fori_loop(0, 8, send, 0)
+            lo, hi = lax.rem(from_z, ZLO), lax.div(from_z, ZLO)
+            for side in range(2):
+                tile = final.at[part, lo * 2 + side]
+                to_lo, to_core = (lo, 1) if side == 0 else (lax.rem(lo + 1, ZLO), 0)
+
+                def send():
+                    pltpu.make_async_remote_copy(
+                        src_ref=tile,
+                        dst_ref=out_ref.at[:, column(head)],
+                        send_sem=send_sem.at[8],
+                        recv_sem=f_sem,
+                        device_id=(to_lo * 2 + to_core, (x * 4 + y) * 4 + hi),
+                        device_id_type=MESH,
+                    ).start()
+
+                def keep():
+                    pltpu.make_async_copy(tile, out_ref.at[:, column(head)], f_sem).start()
+
+                if part < 2:
+                    send()
+                else:
+                    here = jnp.logical_and(hi * ZLO + to_lo == z, core == to_core)
+                    pl.when(jnp.logical_not(here))(send)
+                    pl.when(here)(keep)
 
     peaks = score(0)
     v_cat[:, HEAD:] = jnp.ones((GROUPS * BLOCK, HEAD), jnp.bfloat16)
@@ -288,14 +285,12 @@
     attend(1, score(1))
     attend(2, score(2))
     merge(0)
-    give(0, True)
+    give(0)
     attend(3, score(3))
     sent += [(part_in, 6), (stats.at[:, others], 7), (k_in.at[:, pl.ds(0, (2 * Z - 1) * HEAD)], 8)]
     for part in range(1, PARTS):
         merge(part)
-        give(part, True)
-    for part in range(PARTS):
-        give(part, False)
+        give(part)
     for ref, number in sent:
         wait_bytes(ref, send_sem.at[number])
     wait_bytes(out_ref, f_sem)

time: 60.8 us -> 59.4 us (0.977)
  Pallas kernels: 59.1 us -> 57.7 us
    pallas_call x1, Pallas kernels: 59.1 us -> 57.7 us  [local(): pl.pallas_call(kernel, out_shape=jax.ShapeDtypeStruct((TOK, HEADS * HEAD)...]
where the time goes in v4:
time: 59.4 us; the launch traced here: 59.2 us
  Pallas kernels  57.7 us (97%)
  local copies, waits for them, and re-layouts  1.57 us (3%)
    pallas_call x1, Pallas kernels, local(): pl.pallas_call(kernel, out_shape=jax.ShapeDtypeStruct((TOK, HEADS * HEAD)...  57.7 us
    unnamed x1, local copies, waits for them, and re-layouts  1.57 us

profile of v4, /device:TPU:1, one launch (start us, length us, event | category | flops | bytes accessed | tf_op | source)
XLA Modules:
  0.0 59.2 jit_solution(13319358677101402717)
XLA Ops:
  0.0 57.7 %shard_map.64 = bf16[16,4096]{1,0:T(8,128)(2,1)} custom-call(s32[8]{0:T(128)} %levels_ref.1, s32[8]{0:T(128)} %ids_ref.1, bf16[16,4096]{1,0:T(8,128)(2,1)} %q_ref.1, bf16[16,4096]{1,0:T(8,128)(2,1)} %k_ref.1, bf16[16,4096]{1,0:T(8,128)(2,1)} %v_ref.1, f32[32,4096]{1,0:T(8,128)} %gate_ref.1), custom_call_target="tpu_custom_call" | custom-call | tf_op jit(solution)/shard_map/pallas_call | solution.py:303
  57.7 1.6 %copy.8 = bf16[16,4096]{1,0:T(8,128)(2,1)} copy(bf16[16,4096]{1,0:T(8,128)(2,1)} %shard_map.64) | data formatting | bytes 262144

commit v5 on v4

--- a/solution.py
+++ b/solution.py
@@ -304,7 +304,7 @@
         kernel,
         out_shape=jax.ShapeDtypeStruct((TOK, HEADS * HEAD), bf16),
         in_specs=[pl.BlockSpec(memory_space=pltpu.SMEM)] * 2 + [pl.BlockSpec(memory_space=pl.ANY)] * 4,
-        out_specs=pl.BlockSpec(memory_space=pltpu.VMEM),
+        out_specs=pl.BlockSpec(memory_space=pl.ANY),
         scratch_shapes=[
             pltpu.VMEM((TOK, HEADS * HEAD), bf16),
             pltpu.VMEM((TOK, HEADS * HEAD), bf16),

time: 59.4 us -> 59 us (level)
  no operation moved by 1% of the time
where the time goes in v5:
time: 59 us; the launch traced here: 58.8 us
  Pallas kernels  57.3 us (97%)
  local copies, waits for them, and re-layouts  1.57 us (3%)
    pallas_call x1, Pallas kernels, local(): pl.pallas_call(kernel, out_shape=jax.ShapeDtypeStruct((TOK, HEADS * HEAD)...  57.3 us
    unnamed x1, local copies, waits for them, and re-layouts  1.57 us

profile of v5, /device:TPU:1, one launch (start us, length us, event | category | flops | bytes accessed | tf_op | source)
XLA Modules:
  0.0 58.8 jit_solution(3830634753685973428)
XLA Ops:
  0.0 57.3 %shard_map.64 = bf16[16,4096]{1,0:T(8,128)(2,1)} custom-call(s32[8]{0:T(128)} %levels_ref.1, s32[8]{0:T(128)} %ids_ref.1, bf16[16,4096]{1,0:T(8,128)(2,1)} %q_ref.1, bf16[16,4096]{1,0:T(8,128)(2,1)} %k_ref.1, bf16[16,4096]{1,0:T(8,128)(2,1)} %v_ref.1, f32[32,4096]{1,0:T(8,128)} %gate_ref.1), custom_call_target="tpu_custom_call" | custom-call | tf_op jit(solution)/shard_map/pallas_call | solution.py:303
  57.3 1.6 %copy.8 = bf16[16,4096]{1,0:T(8,128)(2,1)} copy(bf16[16,4096]{1,0:T(8,128)(2,1)} %shard_map.64) | data formatting | bytes 262144
